TPU v7x, 32 devices: a whole 2x2x4 slice. The times are simulated.
32 devices in a mesh: groups: 2 (over y), dp: 4 (over x, core), expert: 4 (over z).
Axes of the slice: x: 2, y: 2, z: 4, core: 2. Of those that a mesh axis runs over, the one named last changes fastest.
Arguments:
- tokens: bfloat16 [256, 2048], P(('groups', 'dp', 'expert')), parts along dimension 0, may hold values from -3.5 to 3.5
- routes: int32 [256, 8], P('groups'), parts along dimension 0, may hold values from 0 to 15, all different within a row; in each aligned block of 8 rows (0 to 7, 8 to 15, ...) at most 8 rows name the same one
- gates: float32 [256, 8], P(('groups', 'dp', 'expert')), parts along dimension 0, may hold values from 0.1 to 1
- valid: int32 [256], P('groups'), parts along dimension 0, may hold values 0 or 1
- norm_gain: float32 [2048], replicated, may hold values from 0.5 to 1.5
- final_gain: float32 [2048], replicated, may hold values from 0.5 to 1.5
- w_gate: bfloat16 [16, 2048, 1024], P('expert', None, 'dp'), may hold values from -0.125 to 0.125
- w_up: bfloat16 [16, 2048, 1024], P('expert', None, 'dp'), may hold values from -0.125 to 0.125
- w_down: bfloat16 [16, 1024, 2048], P('expert', 'dp'), may hold values from -0.1875 to 0.1875
- head_weight: bfloat16 [2048, 10240], P(None, ('dp', 'expert')), as said below
- student_logits: bfloat16 [256, 10240], P('groups', ('dp', 'expert')), parts along dimension 0, may hold values from -24 to 220
Outputs:
- reverse_kl: float32 [256], P('groups'), parts along dimension 0
- logit_grad: bfloat16 [256, 10240], P('groups', ('dp', 'expert')), parts along dimension 0
There are 2 independent parts, one for each index of `groups`. A program takes and returns all parts, laid end to end along the dimension named above; an argument that names none is the same for every part. Nothing has to cross between parts.
Inputs may be any that keep to these rules, and one draw needn't show every extreme that they name: Each token names 8 different experts. In the 8 tokens of one device (aligned blocks of rows), no expert is named by more than 8 routes, a bound that some block reaches. `head_weight`: entries are of order one over the square root of 2048.
All inputs are finite; a program needn't handle non-finite values.
Results may differ from a plain program's by a relative error of at most 0.015.
Values may be sent and summed in bfloat16 or wider, within the bound.
A program may use at most 64 MiB of HBM per device.

v0:
```python
import jax
import jax.numpy as jnp
from jax import lax
from jax.sharding import PartitionSpec as P

epsilon = 1e-06


def rms_scale(values, gain_vector):
    mean_square = jnp.mean(values * values, axis=-1, keepdims=True)
    return values * lax.rsqrt(mean_square + epsilon) * gain_vector


def slot_table(route_rows, expert_count, capacity):
    block_count, tok_count, route_count = route_rows.shape
    flat_routes = route_rows.reshape(block_count, tok_count * route_count)
    experts_iota = jnp.arange(expert_count, dtype=jnp.int32)
    onehot = (flat_routes[:, :, None] == experts_iota[None, None, :]).astype(jnp.int32)
    earlier = jnp.cumsum(onehot, axis=1) - onehot
    slot_rank = jnp.sum(earlier * onehot, axis=2)
    slot_index = flat_routes * capacity + slot_rank
    slots_iota = jnp.arange(expert_count * capacity, dtype=jnp.int32)
    slot_hot = (slot_index[:, :, None] == slots_iota[None, None, :]).astype(jnp.float32)
    return slot_hot.reshape(block_count, tok_count, route_count, expert_count * capacity)


def body(
    tokens,
    routes,
    gates,
    valid,
    norm_gain,
    final_gain,
    w_gate,
    w_up,
    w_down,
    head_weight,
    student_logits,
):
    token_count = tokens.shape[0]
    feature_count = tokens.shape[1]
    route_count = routes.shape[1]
    expert_ranks = lax.axis_size("expert")
    local_experts = w_gate.shape[0]
    expert_count = local_experts * expert_ranks
    capacity = max(2, 2 * token_count * route_count // expert_count)
    slot_total = expert_count * capacity
    hidden_in = tokens.astype(jnp.float32)
    normed = rms_scale(hidden_in, norm_gain).astype(jnp.bfloat16)
    position = lax.axis_index(("dp", "expert"))
    own_routes = lax.dynamic_slice_in_dim(routes, position * token_count, token_count, 0)
    own_hot = slot_table(own_routes[None], expert_count, capacity)[0]
    placed = jnp.einsum(
        "tks,td->sd", own_hot.astype(jnp.bfloat16), normed, preferred_element_type=jnp.float32
    ).astype(jnp.bfloat16)
    placed = placed.reshape(expert_ranks, local_experts, capacity, feature_count)
    received = lax.all_to_all(placed, "expert", split_axis=0, concat_axis=0, tiled=True)
    gathered = lax.all_gather(received, "dp", axis=0, tiled=True)
    gate_part = jnp.einsum("rlcd,ldf->rlcf", gathered, w_gate, preferred_element_type=jnp.float32)
    up_part = jnp.einsum("rlcd,ldf->rlcf", gathered, w_up, preferred_element_type=jnp.float32)
    activation = (jax.nn.silu(gate_part) * up_part).astype(jnp.bfloat16)
    partial_out = lax.psum_scatter(
        jnp.einsum("rlcf,lfd->rlcd", activation, w_down, preferred_element_type=jnp.float32).astype(
            jnp.bfloat16
        ),
        "dp",
        scatter_dimension=0,
        tiled=True,
    )
    returned = lax.all_to_all(partial_out, "expert", split_axis=0, concat_axis=0, tiled=True)
    returned = returned.reshape(slot_total, feature_count).astype(jnp.float32)
    weights = gates / jnp.sum(gates, axis=1, keepdims=True)
    combine_map = jnp.einsum("tk,tks->ts", weights, own_hot, precision=lax.Precision.HIGHEST)
    combined = jnp.dot(combine_map, returned, precision=lax.Precision.HIGHEST)
    mixed = hidden_in + combined
    final_normed = rms_scale(mixed, final_gain).astype(jnp.bfloat16)
    teacher = jnp.dot(
        lax.all_gather(final_normed, ("dp", "expert"), axis=0, tiled=True),
        head_weight,
        preferred_element_type=jnp.float32,
    )
    student = student_logits.astype(jnp.float32)
    teacher_top, student_top = lax.pmax(
        (jnp.max(teacher, axis=1), jnp.max(student, axis=1)), ("dp", "expert")
    )
    teacher_exp = jnp.exp(teacher - teacher_top[:, None])
    student_exp = jnp.exp(student - student_top[:, None])
    local_sums = (
        jnp.sum(teacher_exp, axis=1),
        jnp.sum(student_exp, axis=1),
        jnp.sum(student_exp * (student - teacher), axis=1),
    )
    teacher_total, student_total, cross_term = lax.psum(
        (local_sums[0], local_sums[1], local_sums[2]), ("dp", "expert")
    )
    log_teacher = (teacher_top + jnp.log(teacher_total))[:, None]
    log_student = (student_top + jnp.log(student_total))[:, None]
    divergence = (cross_term / student_total)[:, None] - log_student + log_teacher
    student_prob = jnp.exp(student - log_student)
    valid_rows = valid.astype(jnp.float32)[:, None]
    logit_grad = (
        valid_rows * student_prob * (student - log_student - (teacher - log_teacher) - divergence)
    ).astype(jnp.bfloat16)
    return ((valid_rows * divergence)[:, 0], logit_grad)


def solution(mesh):
    placed = (
        P(("groups", "dp", "expert"), None),
        P("groups", None),
        P(("groups", "dp", "expert"), None),
        P("groups"),
        P(),
        P(),
        P("expert", None, "dp"),
        P("expert", None, "dp"),
        P("expert", "dp", None),
        P(None, ("dp", "expert")),
        P("groups", ("dp", "expert")),
    )
    return jax.shard_map(
        body,
        mesh=mesh,
        in_specs=placed,
        out_specs=(P("groups"), P("groups", ("dp", "expert"))),
        check_vma=False,
    )
```

profile of v0, /device:TPU:0, one launch (start us, length us, event | category | flops | bytes accessed | tf_op | source)
XLA Modules:
  0.0 242.6 jit_solution(7114839426524506998)
XLA Ops:
  7.2 0.0 copy-start
  7.2 0.0 all-gather.2.cloned.1.call-start
  7.2 0.9 constant_dynamic-slice_fusion.1
  8.1 0.1 copy.31
  8.2 0.1 eq.46
  8.3 0.1 fusion.49
  8.4 0.1 reduce_window_sum.11
  8.5 0.2 select_reduce_fusion
  8.7 0.1 reduce_sum.76
  8.7 0.1 convert_reduce_fusion
  8.9 0.9 fusion.42
  9.8 1.1 convolution_convert_fusion
  10.9 20.6 %all_to_all.10 = bf16[4,4,8,2048]{3,2,1,0:T(8,128)(2,1)S(1)} all-to-all(bf16[4,4,8,2048]{3,2,1,0:T(8,128)(2,1)S(1)} %bitcast.64), channel_id=1, replica_groups=mesh['groups'=2,'dp'=4,'expert'=4] {'expert'}, dimensions={0} | all-to-all | bytes 1048576 | tf_op jit(solution)/shard_map/all_to_all | solution.py:57
  31.5 0.8 copy.22
  32.3 0.0 all-gather.2.cloned.1.call-update
  32.3 0.0 all-reduce.5.cloned.1.call-start
  32.4 21.8 %all-gather.2.cloned.1.call-done = bf16[16,4,8,2048]{3,2,0,1:T(8,128)(2,1)} async-done(((bf16[4,4,8,2048]{3,2,0,1:T(8,128)(2,1)}), bf16[16,4,8,2048]{3,2,0,1:T(8,128)(2,1)}) %all-gather.2.cloned.1.call-update) | async-done | bytes 2097168 | tf_op jit(solution)/shard_map/all_gather | solution.py:58
  54.2 3.5 %fusion.12 = f32[16,4,8,256]{3,2,0,1:T(8,128)S(1)} fusion(bf16[16,4,8,2048]{3,2,0,1:T(8,128)(2,1)} %all-gather.2.cloned.1.call-done, bf16[4,2048,256]{2,1,0:T(8,128)(2,1)} %param.17), kind=kOutput, calls=%fused_computation.10 | convolution fusion | flops 536870912 | bytes 6815744 | tf_op jit(solution)/shard_map/rlcd,ldf->rlcf/dot_general | solution.py:59
  57.7 0.0 copy-start.6
  57.7 6.7 %fusion.9 = bf16[16,4,8,2048]{3,2,0,1:T(8,128)(2,1)} fusion(bf16[4,256,2048]{2,1,0:T(8,128)(2,1)} %param.19, bf16[16,4,8,2048]{3,2,0,1:T(8,128)(2,1)} %all-gather.2.cloned.1.call-done, bf16[4,2048,256]{2,1,0:T(8,128)(2,1)} %param.18, f32[16,4,8,256]{3,2,0,1:T(8,128)S(1)} %fusion.12), kind=kOutput, calls=%fused_computation.7 | convolution fusion | flops 1075576832 | bytes 13107200 | tf_op jit(solution)/shard_map/rlcf,lfd->rlcd/dot_general | solution.py:63
  64.4 0.0 copy-start.4
  64.4 0.0 all-reduce.5.cloned.1.call-update
  64.5 0.0 copy-done.6
  64.5 0.6 dynamic-slice
  65.7 50.3 %all-reduce.5.cloned.1.call-done = bf16[16,4,8,2048]{3,2,0,1:T(8,128)(2,1)} async-done(((bf16[16,4,8,2048]{3,2,0,1:T(8,128)(2,1)}), bf16[16,4,8,2048]{3,2,0,1:T(8,128)(2,1)}) %all-reduce.5.cloned.1.call-update) | async-done | bytes 2097168
  116.0 1.1 constant_dynamic-slice_fusion
  117.1 0.8 copy.23
  117.9 4.6 %all-to-all-start.1 = ((bf16[4,4,8,2048]{3,2,1,0:T(8,128)(2,1)}), bf16[4,4,8,2048]{3,2,1,0:T(8,128)(2,1)S(1)}, u32[]{:S(2)}, u32[]{:S(2)}) async-start(bf16[4,4,8,2048]{3,2,1,0:T(8,128)(2,1)} %copy.23), calls=%async_computation.1 | async-start | bytes 1048576 | tf_op jit(solution)/shard_map/all_to_all | solution.py:70
  122.5 0.0 copy-done.5
  122.5 0.0 copy-done.3
  122.5 0.1 reduce_sum.74
  122.6 0.0 copy-done.1
  122.6 0.1 reduce_max.23
  122.7 0.1 broadcast_divide_fusion
  122.8 0.2 fusion.48
  123.1 13.9 %all-to-all-done.1 = bf16[4,4,8,2048]{3,2,1,0:T(8,128)(2,1)S(1)} async-done(((bf16[4,4,8,2048]{3,2,1,0:T(8,128)(2,1)}), bf16[4,4,8,2048]{3,2,1,0:T(8,128)(2,1)S(1)}, u32[]{:S(2)}, u32[]{:S(2)}) %all-to-all-start.1) | async-done | bytes 524320 | tf_op jit(solution)/shard_map/all_to_all | solution.py:70
  136.9 0.0 copy-done.2
  136.9 0.4 multiply_reduce_fusion
  137.4 0.0 copy-done.4
  137.4 0.1 multiply_convert_fusion
  137.5 33.8 %all_gather.7 = bf16[128,2048]{1,0:T(8,128)(2,1)S(1)} all-gather(bf16[8,2048]{1,0:T(8,128)(2,1)S(1)} %multiply_convert_fusion), channel_id=1, replica_groups=mesh['groups'=2,'dp'=4,'expert'=4] {'dp','expert'}, dimensions={0}, use_global_device_ids=true | all-gather | bytes 557056 | tf_op jit(solution)/shard_map/all_gather | solution.py:78
  171.2 0.0 copy-done
  171.2 0.7 fusion.52
  171.9 31.3 %all-reduce.2 = (f32[128]{0:T(128)S(1)}, f32[128]{0:T(128)S(1)}) all-reduce(f32[128]{0:T(128)S(1)} %get-tuple-element.16, bf16[128]{0:T(256)(128)(2,1)S(1)} %reduce_max.23), channel_id=1, replica_groups=mesh['groups'=2,'dp'=4,'expert'=4] {'dp','expert'}, use_global_device_ids=true, to_apply=%region_14.15 | all-reduce | flops 256 | bytes 1792 | tf_op jit(solution)/shard_map/pmax | solution.py:83
  203.2 0.3 fusion.40
  203.5 31.0 %all-reduce.1 = (f32[128]{0:T(128)S(1)}, f32[128]{0:T(128)S(1)}, f32[128]{0:T(128)S(1)}) all-reduce(f32[128]{0:T(128)S(1)} %get-tuple-element.3, f32[128]{0:T(128)S(1)} %get-tuple-element.4, f32[128]{0:T(128)S(1)} %get-tuple-element.2), channel_id=1, replica_groups=mesh['groups'=2,'dp'=4,'expert'=4] {'dp','expert'}, use_global_device_ids=true, to_apply=%region_16.17 | all-reduce | flops 384 | bytes 3072 | tf_op jit(solution)/shard_map/psum | solution.py:93
  234.4 0.5 convert_multiply_fusion.2
  234.9 0.8 fusion.35
  (8 shorter events, 0.0 us)
Async XLA Ops:
  7.2 164.1 %copy-start = (bf16[2048,640]{1,0:T(8,128)(2,1)S(1)}, bf16[2048,640]{1,0:T(8,128)(2,1)}, u32[]{:S(2)}) copy-start(bf16[2048,640]{1,0:T(8,128)(2,1)} %param.20) | copy-start | bytes 7864324
  7.2 47.0 %all-gather.2.cloned.1.call-start = ((), (), s32[]{:S(2)}) async-start(), calls=%async_computation.2 | async-start | bytes 2621440 | tf_op jit(solution)/shard_map/all_gather | solution.py:58
  32.3 83.6 %all-reduce.5.cloned.1.call-start = ((), (), s32[]{:S(2)}) async-start(), calls=%async_computation.3 | async-start | bytes 4194304
  57.7 6.7 %copy-start.6 = (u32[32]{0:T(128)S(1)}, u32[32]{0:T(128)}, u32[]{:S(2)}) copy-start(u32[32]{0:T(128)} %constant.39) | copy-start | bytes 388
  64.4 58.1 %copy-start.5 = (s32[128]{0:T(128)S(1)}, s32[128]{0:T(128)}, u32[]{:S(2)}) copy-start(s32[128]{0:T(128)} %param.14) | copy-start | bytes 1540
  64.4 58.1 %copy-start.3 = (f32[8,8]{1,0:T(8,128)S(1)}, f32[8,8]{1,0:T(8,128)}, u32[]{:S(2)}) copy-start(f32[8,8]{1,0:T(8,128)} %param.13) | copy-start | bytes 772
  64.4 58.2 %copy-start.1 = (bf16[128,640]{1,0:T(8,128)(2,1)S(1)}, bf16[128,640]{1,0:T(8,128)(2,1)}, u32[]{:S(2)}) copy-start(bf16[128,640]{1,0:T(8,128)(2,1)} %param.21) | copy-start | bytes 491524
  64.4 72.5 %copy-start.2 = (bf16[8,2048]{1,0:T(8,128)(2,1)S(1)}, bf16[8,2048]{1,0:T(8,128)(2,1)}, u32[]{:S(2)}) copy-start(bf16[8,2048]{1,0:T(8,128)(2,1)} %param.11) | copy-start | bytes 98308
  64.4 72.9 %copy-start.4 = (f32[2048]{0:T(1024)S(1)}, f32[2048]{0:T(1024)}, u32[]{:S(2)}) copy-start(f32[2048]{0:T(1024)} %param.16) | copy-start | bytes 24580
  117.9 19.0 %all-to-all-start.1 = ((bf16[4,4,8,2048]{3,2,1,0:T(8,128)(2,1)}), bf16[4,4,8,2048]{3,2,1,0:T(8,128)(2,1)S(1)}, u32[]{:S(2)}, u32[]{:S(2)}) async-start(bf16[4,4,8,2048]{3,2,1,0:T(8,128)(2,1)} %copy.23), calls=%async_computation.1 | async-start | bytes 1048576 | tf_op jit(solution)/shard_map/all_to_all | solution.py:70
Sparse Core Ops, SparseCore 0:
  32.5 21.6 all-gather.1
  64.6 51.3 all-reduce.4
where the time goes:
time: 243 us
  blocking collectives  117 us (48%)
  waiting for transfers between devices  86 us (35%)
  between operations  14.8 us (6%)
  matrix products  12.6 us (5%)
  starting transfers between devices  4.68 us (2%)
  local copies, waits for them, and re-layouts  4.5 us (2%)
  other arithmetic  3.42 us (1%)
    unnamed x3, waiting for transfers between devices  50.3 us
    all_gather x1, blocking collectives, body(): lax.all_gather(final_normed, ('dp', 'expert'), axis=0, tiled=True)  33.8 us
    pmax x1, blocking collectives, body(): lax.pmax((jnp.max(teacher, axis=1), jnp.max(student, axis=1)), ('dp', 'ex...  31.3 us
    psum x1, blocking collectives, body(): lax.psum((local_sums[0], local_sums[1], local_sums[2]), ('dp', 'expert'))  31 us
    all_gather x1, waiting for transfers between devices, body(): gathered = lax.all_gather(received, 'dp', axis=0, tiled=True)  21.8 us
    all_to_all x1, blocking collectives, body(): lax.all_to_all(placed, 'expert', split_axis=0, concat_axis=0, tiled=True)  20.6 us
    all_to_all x1, waiting for transfers between devices, body(): lax.all_to_all(partial_out, 'expert', split_axis=0, concat_axis=0, tiled=...  13.9 us
    dot_general x1, matrix products, body(): jnp.einsum('rlcf,lfd->rlcd', activation, w_down, preferred_element_type=j...  6.66 us
  transfers between devices with their start and end apart: 3, of which 3 were waited for; matrix products, arithmetic and copies ran while one was open for 0% of the time, Pallas kernels for 0%

commit v1 on v0

v1 whole, which is shorter than its diff:
```python
import functools

import jax
import jax.numpy as jnp
from jax import lax
from jax.experimental import pallas as pl
from jax.experimental.pallas import tpu as pltpu
from jax.sharding import PartitionSpec as P

epsilon = 1e-06
F32, BF16 = jnp.float32, jnp.bfloat16
LANES = 128


def kernel(
    n_dp,
    n_ex,
    tok_ref,
    routes_ref,
    gates_ref,
    valid_ref,
    ng_ref,
    fg_ref,
    wg_hbm,
    wu_hbm,
    wd_hbm,
    hw_hbm,
    st_hbm,
    kl_ref,
    grad_ref,
    wg,
    wu,
    wd,
    hw,
    st,
    xbuf,
    act,
    yb,
    cbuf,
    sbuf,
    rbuf,
    zbuf,
    stat,
    teach,
    load_sem,
    x_send,
    x_recv,
    x_fwd,
    c_send,
    c_recv,
    r_send,
    r_recv,
    z_send,
    z_recv,
    z_fwd,
    s_send,
    s_recv,
):
    grp, dp, ex = lax.axis_index("groups"), lax.axis_index("dp"), lax.axis_index("expert")
    core = lax.rem(dp, 2)
    col = lax.div(dp, 2)
    n_dev = n_dp * n_ex
    n_chip = n_dev // 2
    me = dp * n_ex + ex
    chip = col * n_ex + ex
    per, width = tok_ref.shape
    half = width // 2
    total = n_dev * per
    rows = min(total, 128)
    blocks = rows // per
    local = wg.shape[0]
    hidden = wg.shape[2]

    def device(position):
        return (grp, lax.div(position, n_ex), lax.rem(position, n_ex))

    def at_chip(q, c):
        return (2 * lax.div(q, n_ex) + c) * n_ex + lax.rem(q, n_ex)

    sibling = at_chip(chip, 1 - core)

    def remote(src, dst, send, recv, position):
        return pltpu.make_async_remote_copy(
            src_ref=src,
            dst_ref=dst,
            send_sem=send,
            recv_sem=recv,
            device_id=device(position),
            device_id_type=pl.DeviceIdType.MESH,
        )

    loads = [
        pltpu.make_async_copy(src, dst, load_sem.at[i])
        for i, (src, dst) in enumerate(
            ((wg_hbm, wg), (wu_hbm, wu), (wd_hbm, wd), (st_hbm, st), (hw_hbm, hw))
        )
    ]
    for load in loads:
        load.start()

    barrier = pltpu.get_barrier_semaphore()

    def greet(k, carry):
        pl.semaphore_signal(
            barrier,
            inc=1,
            device_id=device(lax.rem(me + k, n_dev)),
            device_id_type=pl.DeviceIdType.MESH,
        )
        return carry

    lax.fori_loop(1, n_dev, greet, 0)

    x = tok_ref[...].astype(F32)
    normed = x * lax.rsqrt(jnp.mean(x * x, axis=-1, keepdims=True) + epsilon) * ng_ref[...]
    gates = gates_ref[...]
    weights = gates / jnp.sum(gates, axis=1, keepdims=True)
    own_routes = routes_ref[pl.ds(pl.multiple_of(me * per, per), per), :]
    lane = lax.broadcasted_iota(jnp.int32, (per, LANES), 1)
    dense = jnp.zeros((per, LANES), F32)
    for k in range(gates.shape[1]):
        dense += jnp.where(lane == own_routes[:, k : k + 1], weights[:, k : k + 1], 0.0)
    high = dense.astype(BF16).astype(F32)
    xbuf[me, :, 0:half] = jnp.concatenate([normed[:, :half], normed[:, half:]], axis=0).astype(BF16)
    xbuf[me, :, half : half + LANES] = jnp.concatenate([high, dense - high], axis=0).astype(BF16)

    pl.semaphore_wait(barrier, n_dev - 1)

    def gather(buf, send, recv, fwd):
        def direct(k):
            position = at_chip(lax.rem(chip + k, n_chip), core)
            return remote(buf.at[me], buf.at[me], send.at[k], recv.at[me], position)

        to_sibling = remote(buf.at[me], buf.at[me], send.at[0], recv.at[me], sibling)

        def arrival(position):
            return remote(buf.at[position], buf.at[position], send.at[0], recv.at[position], sibling)

        def forward(k):
            position = at_chip(lax.rem(chip + n_chip - k, n_chip), core)
            return remote(buf.at[position], buf.at[position], fwd.at[k], recv.at[position], sibling)

        def start(k, carry):
            direct(k).start()
            return carry

        def relay(k, carry):
            arrival(at_chip(lax.rem(chip + n_chip - k, n_chip), core)).wait_recv()
            forward(k).start()
            return carry

        def collect(k, carry):
            arrival(at_chip(lax.rem(chip + n_chip - k, n_chip), 1 - core)).wait_recv()
            return carry

        def finish(k, carry):
            direct(k).wait_send()
            forward(k).wait_send()
            return carry

        lax.fori_loop(1, n_chip, start, 0)
        to_sibling.start()
        lax.fori_loop(1, n_chip, relay, 0)
        lax.fori_loop(0, n_chip, collect, 0)

        def done():
            to_sibling.wait_send()
            lax.fori_loop(1, n_chip, finish, 0)

        return done

    finish_x = gather(xbuf, x_send, x_recv, x_fwd)

    loads[0].wait()
    loads[1].wait()
    loads[2].wait()

    def experts(r, carry):
        first = pl.multiple_of(r * blocks, blocks)
        packed = xbuf[pl.ds(first, blocks)].astype(F32)
        low = packed[:, 0:per, :].reshape(rows, half + LANES)
        top = packed[:, per : 2 * per, :].reshape(rows, half + LANES)
        inputs = jnp.concatenate([low[:, :half], top[:, :half]], axis=1).astype(BF16)
        scales = low[:, half:] + top[:, half:]
        where = lax.broadcasted_iota(jnp.int32, (rows, LANES), 1)
        for j in range(local):
            scale = jnp.sum(
                jnp.where(where == ex * local + j, scales, 0.0), axis=1, keepdims=True
            )
            gate = jnp.dot(inputs, wg[j], preferred_element_type=F32)
            up = jnp.dot(inputs, wu[j], preferred_element_type=F32)
            out = gate / (1.0 + jnp.exp(-gate)) * up * scale
            act[:, j * hidden : (j + 1) * hidden] = out.astype(BF16)
        step = min(half, 512)
        for n in range(half // step):
            pair = []
            for base in (0, half):
                part = None
                lo = base + n * step
                down = wd[:, :, lo : lo + step].reshape(local * hidden, step)
                part = jnp.dot(act[...], down, preferred_element_type=F32)
                pair.append(part.reshape(blocks, per, step))
            yb[pl.ds(first, blocks), :, n * step : (n + 1) * step] = jnp.concatenate(
                pair, axis=1
            ).astype(BF16)
        return carry

    lax.fori_loop(0, total // rows, experts, 0)

    def half_sum(c):
        src = pl.multiple_of((2 * c + 1 - core) * n_ex, n_ex)
        return remote(
            yb.at[pl.ds(src, n_ex)],
            cbuf.at[pl.ds(pl.multiple_of(c * n_ex, n_ex), n_ex)],
            c_send.at[c],
            c_recv.at[c],
            sibling,
        )

    for c in range(n_dp // 2):
        half_sum(c).start()
    for c in range(n_dp // 2):
        half_sum(c).wait_recv()

    def scatter(k):
        q = lax.rem(chip + k, n_chip)
        return remote(
            sbuf.at[q], rbuf.at[chip], r_send.at[k], r_recv.at[chip], at_chip(q, core)
        )

    def scatter_from(q):
        return remote(sbuf.at[q], rbuf.at[q], r_send.at[0], r_recv.at[q], at_chip(q, core))

    def add_and_send(k, carry):
        q = lax.rem(chip + k, n_chip)
        sbuf[q] = (yb[at_chip(q, core)].astype(F32) + cbuf[q].astype(F32)).astype(BF16)
        scatter(k).start()
        return carry

    lax.fori_loop(1, n_chip, add_and_send, 0)
    mine = yb[me].astype(F32) + cbuf[chip].astype(F32)

    def take(k, acc):
        q = lax.rem(chip + n_chip - k, n_chip)
        scatter_from(q).wait_recv()
        return acc + rbuf[q].astype(F32)

    mine = lax.fori_loop(1, n_chip, take, mine)
    mixed_low = x[:, :half] + mine[:per]
    mixed_top = x[:, half:] + mine[per:]
    square = jnp.sum(mixed_low * mixed_low + mixed_top * mixed_top, axis=-1, keepdims=True)
    inverse = lax.rsqrt(square / width + epsilon)
    zbuf[me] = jnp.concatenate(
        [mixed_low * inverse * fg_ref[:, :half], mixed_top * inverse * fg_ref[:, half:]], axis=0
    ).astype(BF16)

    finish_z = gather(zbuf, z_send, z_recv, z_fwd)
    loads[3].wait()
    loads[4].wait()

    def head(r, carry):
        first = pl.multiple_of(r * blocks, blocks)
        span = pl.ds(pl.multiple_of(r * rows, rows), rows)
        packed = zbuf[pl.ds(first, blocks)].astype(F32)
        low = packed[:, 0:per, :].reshape(rows, half)
        top = packed[:, per : 2 * per, :].reshape(rows, half)
        inputs = jnp.concatenate([low, top], axis=1).astype(BF16)
        teacher = jnp.dot(inputs, hw[...], preferred_element_type=F32)
        teach[span, :] = teacher
        student = st[span, :].astype(F32)
        t_top = jnp.max(teacher, axis=1, keepdims=True)
        s_top = jnp.max(student, axis=1, keepdims=True)
        t_sum = jnp.sum(jnp.exp(teacher - t_top), axis=1, keepdims=True)
        s_exp = jnp.exp(student - s_top)
        s_sum = jnp.sum(s_exp, axis=1, keepdims=True)
        cross = jnp.sum(s_exp * (student - teacher), axis=1, keepdims=True)
        where = lax.broadcasted_iota(jnp.int32, (rows, LANES), 1)
        table = jnp.zeros((rows, LANES), F32)
        for i, value in enumerate((t_top, t_sum, s_top, s_sum, cross)):
            table = jnp.where(where == i, value, table)
        stat[me, :, span] = table.T[0:8]
        return carry

    lax.fori_loop(0, total // rows, head, 0)

    def tell(k):
        position = lax.rem(me + k, n_dev)
        return remote(stat.at[me], stat.at[me], s_send.at[k], s_recv.at[me], position)

    def heard(k):
        position = lax.rem(me + k, n_dev)
        return remote(stat.at[position], stat.at[position], s_send.at[0], s_recv.at[position], sibling)

    def tell_all(k, carry):
        tell(k).start()
        return carry

    def hear_all(k, carry):
        heard(k).wait_recv()
        return carry

    lax.fori_loop(1, n_dev, tell_all, 0)
    lax.fori_loop(1, n_dev, hear_all, 0)

    def final(r, carry):
        span = pl.ds(pl.multiple_of(r * rows, rows), rows)
        t_tops, t_sums = stat[:, 0, span], stat[:, 1, span]
        s_tops, s_sums, crosses = stat[:, 2, span], stat[:, 3, span], stat[:, 4, span]
        t_top = jnp.max(t_tops, axis=0, keepdims=True)
        s_top = jnp.max(s_tops, axis=0, keepdims=True)
        t_total = jnp.sum(jnp.exp(t_tops - t_top) * t_sums, axis=0, keepdims=True)
        s_scale = jnp.exp(s_tops - s_top)
        s_total = jnp.sum(s_scale * s_sums, axis=0, keepdims=True)
        cross = jnp.sum(s_scale * crosses, axis=0, keepdims=True)
        log_t = t_top + jnp.log(t_total)
        log_s = s_top + jnp.log(s_total)
        divergence = cross / s_total - log_s + log_t
        valid = valid_ref[:, span].astype(F32)
        kl_ref[:, span] = valid * divergence
        where = lax.broadcasted_iota(jnp.int32, (LANES, rows), 0)
        table = jnp.zeros((LANES, rows), F32)
        for i, value in enumerate((log_s, divergence - log_t + log_s, valid)):
            table = jnp.where(where == i, value, table)
        columns = table.T
        student = st[span, :].astype(F32)
        prob = columns[:, 2:3] * jnp.exp(student - columns[:, 0:1])
        grad_ref[span, :] = (prob * (student - teach[span, :] - columns[:, 1:2])).astype(BF16)
        return carry

    lax.fori_loop(0, total // rows, final, 0)

    finish_x()
    finish_z()
    for c in range(n_dp // 2):
        half_sum(c).wait_send()

    def finish_scatter(k, carry):
        scatter(k).wait_send()
        return carry

    def finish_tell(k, carry):
        tell(k).wait_send()
        return carry

    lax.fori_loop(1, n_chip, finish_scatter, 0)
    lax.fori_loop(1, n_dev, finish_tell, 0)


def body(
    n_dp,
    n_ex,
    tokens,
    routes,
    gates,
    valid,
    norm_gain,
    final_gain,
    w_gate,
    w_up,
    w_down,
    head_weight,
    student_logits,
):
    per, width = tokens.shape
    half = width // 2
    n_dev = n_dp * n_ex
    n_chip = n_dev // 2
    total, vocab = student_logits.shape
    local, _, hidden = w_gate.shape
    rows = min(total, 128)
    vmem = pl.BlockSpec(memory_space=pltpu.VMEM)
    hbm = pl.BlockSpec(memory_space=pl.ANY)
    dma = pltpu.SemaphoreType.DMA
    kl, grad = pl.pallas_call(
        functools.partial(kernel, n_dp, n_ex),
        out_shape=(
            jax.ShapeDtypeStruct((1, total), F32),
            jax.ShapeDtypeStruct((total, vocab), BF16),
        ),
        in_specs=[vmem] * 6 + [hbm] * 5,
        out_specs=(vmem, vmem),
        scratch_shapes=[
            pltpu.VMEM(w_gate.shape, BF16),
            pltpu.VMEM(w_up.shape, BF16),
            pltpu.VMEM(w_down.shape, BF16),
            pltpu.VMEM(head_weight.shape, BF16),
            pltpu.VMEM(student_logits.shape, BF16),
            pltpu.VMEM((n_dev, 2 * per, half + LANES), BF16),
            pltpu.VMEM((rows, local * hidden), BF16),
            pltpu.VMEM((n_dev, 2 * per, half), BF16),
            pltpu.VMEM((n_chip, 2 * per, half), BF16),
            pltpu.VMEM((n_chip, 2 * per, half), BF16),
            pltpu.VMEM((n_chip, 2 * per, half), BF16),
            pltpu.VMEM((n_dev, 2 * per, half), BF16),
            pltpu.VMEM((n_dev, 8, total), F32),
            pltpu.VMEM((total, vocab), F32),
            dma((5,)),
            dma((n_chip,)),
            dma((n_dev,)),
            dma((n_chip,)),
            dma((n_dp // 2,)),
            dma((n_dp // 2,)),
            dma((n_chip,)),
            dma((n_chip,)),
            dma((n_chip,)),
            dma((n_dev,)),
            dma((n_chip,)),
            dma((n_dev,)),
            dma((n_dev,)),
        ],
        compiler_params=pltpu.CompilerParams(
            collective_id=0, has_side_effects=True, vmem_limit_bytes=60 * 2**20
        ),
    )(
        tokens,
        routes,
        gates,
        valid.reshape(1, total),
        norm_gain.reshape(1, width),
        final_gain.reshape(1, width),
        w_gate,
        w_up,
        w_down,
        head_weight,
        student_logits,
    )
    return kl.reshape(total), grad


def solution(mesh):
    placed = (
        P(("groups", "dp", "expert"), None),
        P("groups", None),
        P(("groups", "dp", "expert"), None),
        P("groups"),
        P(),
        P(),
        P("expert", None, "dp"),
        P("expert", None, "dp"),
        P("expert", "dp", None),
        P(None, ("dp", "expert")),
        P("groups", ("dp", "expert")),
    )
    return jax.shard_map(
        functools.partial(body, mesh.shape["dp"], mesh.shape["expert"]),
        mesh=mesh,
        in_specs=placed,
        out_specs=(P("groups"), P("groups", ("dp", "expert"))),
        check_vma=False,
    )
```

time: 243 us -> 45.6 us (0.19)
  blocking collectives: 117 us -> 0 us
  waiting for transfers between devices: 86 us -> 0 us
  Pallas kernels: 0 us -> 40.6 us
  between operations: 14.8 us -> 0.64 us
  matrix products: 12.6 us -> 0 us
  starting transfers between devices: 4.68 us -> 0 us
  other arithmetic: 3.42 us -> 0 us
    unnamed x3 -> x0, waiting for transfers between devices: 50.3 us -> none
    pallas_call x0 -> x1, Pallas kernels: none -> 40.6 us  [body(): pl.pallas_call(functools.partial(kernel, n_dp, n_ex), out_shape=(jax.Shap...]
    all_gather x1 -> x0, blocking collectives: 33.8 us -> none  [body(): lax.all_gather(final_normed, ('dp', 'expert'), axis=0, tiled=True)]
    pmax x1 -> x0, blocking collectives: 31.3 us -> none  [body(): lax.pmax((jnp.max(teacher, axis=1), jnp.max(student, axis=1)), ('dp', 'ex...]
    psum x1 -> x0, blocking collectives: 31 us -> none  [body(): lax.psum((local_sums[0], local_sums[1], local_sums[2]), ('dp', 'expert'))]
    all_gather x1 -> x0, waiting for transfers between devices: 21.8 us -> none  [body(): gathered = lax.all_gather(received, 'dp', axis=0, tiled=True)]
    all_to_all x1 -> x0, blocking collectives: 20.6 us -> none  [body(): lax.all_to_all(placed, 'expert', split_axis=0, concat_axis=0, tiled=True)]
    all_to_all x1 -> x0, waiting for transfers between devices: 13.9 us -> none  [body(): lax.all_to_all(partial_out, 'expert', split_axis=0, concat_axis=0, tiled=...]
  transfers between devices with their start and end apart: 3 -> 0, of which waited for: 3 -> 0; matrix products, arithmetic and copies ran while one was open for 0% -> 0% of each run, Pallas kernels for 0% -> 0%
where the time goes in v1:
time: 45.6 us; the launch traced here: 45.3 us
  Pallas kernels  40.6 us (89%)
  local copies, waits for them, and re-layouts  4.15 us (9%)
  between operations  0.64 us (1%)
    pallas_call x1, Pallas kernels, body(): pl.pallas_call(functools.partial(kernel, n_dp, n_ex), out_shape=(jax.Shap...  40.6 us
    unnamed x3, local copies, waits for them, and re-layouts  4.15 us

profile of v1, /device:TPU:0, one launch (start us, length us, event | category | flops | bytes accessed | tf_op | source)
XLA Modules:
  0.0 45.3 jit_solution(2843143712154643284)
XLA Ops:
  0.6 1.4 %copy.13.routes_ref = s32[128,8]{1,0:T(8,128)} copy(s32[128,8]{0,1:T(8,128)} %param.12) | data formatting | bytes 8192 | tf_op args[1]
  2.0 40.6 %shard_map.122 = (f32[1,128]{1,0:T(1,128)}, bf16[128,640]{1,0:T(8,128)(2,1)}) custom-call(bf16[8,2048]{1,0:T(8,128)(2,1)} %tok_ref.1, s32[128,8]{1,0:T(8,128)} %copy.13.routes_ref, f32[8,8]{1,0:T(8,128)} %gates_ref.1, s32[1,128]{1,0:T(1,128)} %bitcast.6, f32[1,2048]{1,0:T(1,128)} %bitcast.4, f32[1,2048]{1,0:T(1,128)} %bitcast.5, ...), custom_call_target="tpu_custom_call" | custom-call | tf_op jit(solution)/shard_map/pallas_call | solution.py:374
  42.6 1.1 %copy.16 = f32[128]{0:T(128)} copy(f32[128]{0:T(128)} %bitcast.7) | data formatting | bytes 1024
  43.7 1.6 %copy.17 = bf16[128,640]{1,0:T(8,128)(2,1)} copy(bf16[128,640]{1,0:T(8,128)(2,1)} %get-tuple-element.9) | data formatting | bytes 327680

commit v2 on v1

--- a/solution.py
+++ b/solution.py
@@ -37,22 +37,28 @@
     act,
     yb,
     cbuf,
-    sbuf,
-    rbuf,
+    sxbuf,
+    rxbuf,
+    szbuf,
+    rzbuf,
     zbuf,
     stat,
     teach,
     load_sem,
-    x_send,
+    x_z,
+    x_x,
+    x_c,
     x_recv,
-    x_fwd,
     c_send,
     c_recv,
-    r_send,
-    r_recv,
-    z_send,
+    rx_send,
+    rx_recv,
+    rz_send,
+    rz_recv,
+    z_z,
+    z_x,
+    z_c,
     z_recv,
-    z_fwd,
     s_send,
     s_recv,
 ):
@@ -60,9 +66,8 @@
     core = lax.rem(dp, 2)
     col = lax.div(dp, 2)
     n_dev = n_dp * n_ex
-    n_chip = n_dev // 2
+    n_col = n_dp // 2
     me = dp * n_ex + ex
-    chip = col * n_ex + ex
     per, width = tok_ref.shape
     half = width // 2
     total = n_dev * per
@@ -74,10 +79,21 @@
     def device(position):
         return (grp, lax.div(position, n_ex), lax.rem(position, n_ex))
 
-    def at_chip(q, c):
-        return (2 * lax.div(q, n_ex) + c) * n_ex + lax.rem(q, n_ex)
-
-    sibling = at_chip(chip, 1 - core)
+    def at(x_col, c, z):
+        return (2 * x_col + c) * n_ex + z
+
+    def col_at(k):
+        return lax.rem(col + k, n_col)
+
+    def z_at(k):
+        out, bit = ex, 1
+        while bit < n_ex:
+            if k & bit:
+                out = out + bit - 2 * bit * lax.rem(lax.div(ex, bit), 2)
+            bit *= 2
+        return out
+
+    sibling = at(col, 1 - core, ex)
 
     def remote(src, dst, send, recv, position):
         return pltpu.make_async_remote_copy(
@@ -115,61 +131,59 @@
     normed = x * lax.rsqrt(jnp.mean(x * x, axis=-1, keepdims=True) + epsilon) * ng_ref[...]
     gates = gates_ref[...]
     weights = gates / jnp.sum(gates, axis=1, keepdims=True)
-    own_routes = routes_ref[pl.ds(pl.multiple_of(me * per, per), per), :]
     lane = lax.broadcasted_iota(jnp.int32, (per, LANES), 1)
+    spot = lax.broadcasted_iota(jnp.int32, (per, total), 1)
+    own = spot == lax.broadcasted_iota(jnp.int32, (per, total), 0) + me * per
     dense = jnp.zeros((per, LANES), F32)
     for k in range(gates.shape[1]):
-        dense += jnp.where(lane == own_routes[:, k : k + 1], weights[:, k : k + 1], 0.0)
+        route = jnp.sum(
+            jnp.where(own, routes_ref[k : k + 1, :], 0).astype(F32), axis=1, keepdims=True
+        )
+        dense += jnp.where(lane.astype(F32) == route, weights[:, k : k + 1], 0.0)
     high = dense.astype(BF16).astype(F32)
     xbuf[me, :, 0:half] = jnp.concatenate([normed[:, :half], normed[:, half:]], axis=0).astype(BF16)
     xbuf[me, :, half : half + LANES] = jnp.concatenate([high, dense - high], axis=0).astype(BF16)
 
     pl.semaphore_wait(barrier, n_dev - 1)
 
-    def gather(buf, send, recv, fwd):
-        def direct(k):
-            position = at_chip(lax.rem(chip + k, n_chip), core)
-            return remote(buf.at[me], buf.at[me], send.at[k], recv.at[me], position)
-
-        to_sibling = remote(buf.at[me], buf.at[me], send.at[0], recv.at[me], sibling)
-
-        def arrival(position):
-            return remote(buf.at[position], buf.at[position], send.at[0], recv.at[position], sibling)
-
-        def forward(k):
-            position = at_chip(lax.rem(chip + n_chip - k, n_chip), core)
-            return remote(buf.at[position], buf.at[position], fwd.at[k], recv.at[position], sibling)
-
-        def start(k, carry):
-            direct(k).start()
-            return carry
-
-        def relay(k, carry):
-            arrival(at_chip(lax.rem(chip + n_chip - k, n_chip), core)).wait_recv()
-            forward(k).start()
-            return carry
-
-        def collect(k, carry):
-            arrival(at_chip(lax.rem(chip + n_chip - k, n_chip), 1 - core)).wait_recv()
-            return carry
-
-        def finish(k, carry):
-            direct(k).wait_send()
-            forward(k).wait_send()
-            return carry
-
-        lax.fori_loop(1, n_chip, start, 0)
-        to_sibling.start()
-        lax.fori_loop(1, n_chip, relay, 0)
-        lax.fori_loop(0, n_chip, collect, 0)
-
-        def done():
-            to_sibling.wait_send()
-            lax.fori_loop(1, n_chip, finish, 0)
-
-        return done
-
-    finish_x = gather(xbuf, x_send, x_recv, x_fwd)
+    def gather(buf, send_z, send_x, send_c, recv):
+        def move(position, sem, target):
+            return remote(buf.at[position], buf.at[position], sem, recv.at[position], target)
+
+        started = []
+
+        def start(position, sem, target):
+            copy = move(position, sem, target)
+            copy.start()
+            started.append(copy)
+
+        def arrive(position):
+            move(position, send_c.at[0], sibling).wait_recv()
+
+        def to_columns(position, kz):
+            for kx in range(1, n_col):
+                start(position, send_x.at[kz * n_col + kx], at(col_at(kx), core, ex))
+
+        to_columns(me, 0)
+        for kz in range(n_ex - 1, 0, -1):
+            start(me, send_z.at[kz], at(col, core, z_at(kz)))
+        start(me, send_c.at[0], sibling)
+        for kz in range(1, n_ex):
+            position = at(col, core, z_at(kz))
+            arrive(position)
+            to_columns(position, kz)
+            start(position, send_c.at[kz * n_col], sibling)
+        for kz in range(n_ex):
+            for kx in range(1, n_col):
+                position = at(col_at(n_col - kx), core, z_at(kz))
+                arrive(position)
+                start(position, send_c.at[kz * n_col + kx], sibling)
+        for kz in range(n_ex):
+            for kx in range(n_col):
+                arrive(at(col_at(n_col - kx), 1 - core, z_at(kz)))
+        return started
+
+    sent = gather(xbuf, x_z, x_x, x_c, x_recv)
 
     loads[0].wait()
     loads[1].wait()
@@ -207,45 +221,58 @@
 
     lax.fori_loop(0, total // rows, experts, 0)
 
-    def half_sum(c):
+    def half_sum(kx):
+        c = col_at(kx)
         src = pl.multiple_of((2 * c + 1 - core) * n_ex, n_ex)
         return remote(
             yb.at[pl.ds(src, n_ex)],
             cbuf.at[pl.ds(pl.multiple_of(c * n_ex, n_ex), n_ex)],
-            c_send.at[c],
-            c_recv.at[c],
+            c_send.at[kx],
+            c_recv.at[kx],
             sibling,
         )
 
-    for c in range(n_dp // 2):
-        half_sum(c).start()
-    for c in range(n_dp // 2):
-        half_sum(c).wait_recv()
-
-    def scatter(k):
-        q = lax.rem(chip + k, n_chip)
-        return remote(
-            sbuf.at[q], rbuf.at[chip], r_send.at[k], r_recv.at[chip], at_chip(q, core)
-        )
-
-    def scatter_from(q):
-        return remote(sbuf.at[q], rbuf.at[q], r_send.at[0], r_recv.at[q], at_chip(q, core))
-
-    def add_and_send(k, carry):
-        q = lax.rem(chip + k, n_chip)
-        sbuf[q] = (yb[at_chip(q, core)].astype(F32) + cbuf[q].astype(F32)).astype(BF16)
-        scatter(k).start()
-        return carry
-
-    lax.fori_loop(1, n_chip, add_and_send, 0)
-    mine = yb[me].astype(F32) + cbuf[chip].astype(F32)
-
-    def take(k, acc):
-        q = lax.rem(chip + n_chip - k, n_chip)
-        scatter_from(q).wait_recv()
-        return acc + rbuf[q].astype(F32)
-
-    mine = lax.fori_loop(1, n_chip, take, mine)
+    def pair_sum(kx, kz):
+        c, z = col_at(kx), z_at(kz)
+        return yb[at(c, core, z)].astype(F32) + cbuf[c * n_ex + z].astype(F32)
+
+    column_order = [*range(1, n_col), 0]
+    for kx in column_order:
+        half_sum(kx).start()
+    for kx in range(1, n_col):
+        half_sum(kx).wait_recv()
+        sent.append(half_sum(kx))
+        for kz in range(n_ex - 1, -1, -1):
+            i = kx * n_ex + kz
+            sxbuf[i] = pair_sum(kx, kz).astype(BF16)
+            copy = remote(
+                sxbuf.at[i], rxbuf.at[i], rx_send.at[i], rx_recv.at[i], at(col_at(kx), core, ex)
+            )
+            copy.start()
+            sent.append(copy)
+    half_sum(0).wait_recv()
+    sent.append(half_sum(0))
+    mine = None
+    for kz in range(n_ex - 1, -1, -1):
+        mine = pair_sum(0, kz)
+        for kx in range(1, n_col):
+            i = kx * n_ex + kz
+            remote(
+                sxbuf.at[i], rxbuf.at[i], rx_send.at[i], rx_recv.at[i], at(col_at(kx), core, ex)
+            ).wait_recv()
+            mine += rxbuf[i].astype(F32)
+        if kz:
+            szbuf[kz] = mine.astype(BF16)
+            copy = remote(
+                szbuf.at[kz], rzbuf.at[kz], rz_send.at[kz], rz_recv.at[kz], at(col, core, z_at(kz))
+            )
+            copy.start()
+            sent.append(copy)
+    for kz in range(1, n_ex):
+        remote(
+            szbuf.at[kz], rzbuf.at[kz], rz_send.at[kz], rz_recv.at[kz], at(col, core, z_at(kz))
+        ).wait_recv()
+        mine += rzbuf[kz].astype(F32)
     mixed_low = x[:, :half] + mine[:per]
     mixed_top = x[:, half:] + mine[per:]
     square = jnp.sum(mixed_low * mixed_low + mixed_top * mixed_top, axis=-1, keepdims=True)
@@ -254,7 +281,7 @@
         [mixed_low * inverse * fg_ref[:, :half], mixed_top * inverse * fg_ref[:, half:]], axis=0
     ).astype(BF16)
 
-    finish_z = gather(zbuf, z_send, z_recv, z_fwd)
+    sent += gather(zbuf, z_z, z_x, z_c, z_recv)
     loads[3].wait()
     loads[4].wait()
 
@@ -329,20 +356,13 @@
 
     lax.fori_loop(0, total // rows, final, 0)
 
-    finish_x()
-    finish_z()
-    for c in range(n_dp // 2):
-        half_sum(c).wait_send()
-
-    def finish_scatter(k, carry):
-        scatter(k).wait_send()
-        return carry
+    for copy in sent:
+        copy.wait_send()
 
     def finish_tell(k, carry):
         tell(k).wait_send()
         return carry
 
-    lax.fori_loop(1, n_chip, finish_scatter, 0)
     lax.fori_loop(1, n_dev, finish_tell, 0)
 
 
@@ -365,6 +385,7 @@
     half = width // 2
     n_dev = n_dp * n_ex
     n_chip = n_dev // 2
+    n_col = n_dp // 2
     total, vocab = student_logits.shape
     local, _, hidden = w_gate.shape
     rows = min(total, 128)
@@ -391,20 +412,26 @@
             pltpu.VMEM((n_chip, 2 * per, half), BF16),
             pltpu.VMEM((n_chip, 2 * per, half), BF16),
             pltpu.VMEM((n_chip, 2 * per, half), BF16),
+            pltpu.VMEM((n_ex, 2 * per, half), BF16),
+            pltpu.VMEM((n_ex, 2 * per, half), BF16),
             pltpu.VMEM((n_dev, 2 * per, half), BF16),
             pltpu.VMEM((n_dev, 8, total), F32),
             pltpu.VMEM((total, vocab), F32),
             dma((5,)),
+            dma((n_ex,)),
+            dma((n_chip,)),
             dma((n_chip,)),
             dma((n_dev,)),
-            dma((n_chip,)),
-            dma((n_dp // 2,)),
-            dma((n_dp // 2,)),
-            dma((n_chip,)),
+            dma((n_col,)),
+            dma((n_col,)),
+            dma((n_chip,)),
+            dma((n_chip,)),
+            dma((n_ex,)),
+            dma((n_ex,)),
+            dma((n_ex,)),
             dma((n_chip,)),
             dma((n_chip,)),
             dma((n_dev,)),
-            dma((n_chip,)),
             dma((n_dev,)),
             dma((n_dev,)),
         ],
@@ -413,7 +440,7 @@
         ),
     )(
         tokens,
-        routes,
+        routes.T,
         gates,
         valid.reshape(1, total),
         norm_gain.reshape(1, width),

time: 45.6 us -> 45 us (0.987)
  local copies, waits for them, and re-layouts: 4.15 us -> 2.73 us
  Pallas kernels: 40.6 us -> 41.4 us
    unnamed x3 -> x2, local copies, waits for them, and re-layouts: 4.15 us -> 2.73 us
    pallas_call x1, Pallas kernels: 40.6 us -> 41.4 us  [body(): pl.pallas_call(functools.partial(kernel, n_dp, n_ex), out_shape=(jax.Shap...]
where the time goes in v2:
time: 45 us; the launch traced here: 44.8 us
  Pallas kernels  41.4 us (92%)
  local copies, waits for them, and re-layouts  2.73 us (6%)
  between operations  0.64 us (1%)
    pallas_call x1, Pallas kernels, body(): pl.pallas_call(functools.partial(kernel, n_dp, n_ex), out_shape=(jax.Shap...  41.4 us
    unnamed x2, local copies, waits for them, and re-layouts  2.73 us

profile of v2, /device:TPU:0, one launch (start us, length us, event | category | flops | bytes accessed | tf_op | source)
XLA Modules:
  0.0 44.8 jit_solution(6185705407395503237)
XLA Ops:
  0.6 41.4 %shard_map.122 = (f32[1,128]{1,0:T(1,128)}, bf16[128,640]{1,0:T(8,128)(2,1)}) custom-call(bf16[8,2048]{1,0:T(8,128)(2,1)} %tok_ref.1, s32[8,128]{1,0:T(8,128)} %bitcast.7, f32[8,8]{1,0:T(8,128)} %gates_ref.1, s32[1,128]{1,0:T(1,128)} %bitcast.8, f32[1,2048]{1,0:T(1,128)} %bitcast.5, f32[1,2048]{1,0:T(1,128)} %bitcast.6, bf16[4,2048,256]{2,1,0:T(8,128)(2,1)} %wg_hbm.1, ...), custom_call_target="tpu_custom_call" | custom-call | tf_op jit(solution)/shard_map/pallas_call | solution.py:395
  42.1 1.1 %copy.15 = f32[128]{0:T(128)} copy(f32[128]{0:T(128)} %bitcast.9) | data formatting | bytes 1024
  43.2 1.6 %copy.16 = bf16[128,640]{1,0:T(8,128)(2,1)} copy(bf16[128,640]{1,0:T(8,128)(2,1)} %get-tuple-element.9) | data formatting | bytes 327680

commit v3 on v2

--- a/solution.py
+++ b/solution.py
@@ -26,8 +26,8 @@
     wd_hbm,
     hw_hbm,
     st_hbm,
-    kl_ref,
-    grad_ref,
+    teach,
+    facts,
     wg,
     wu,
     wd,
@@ -39,11 +39,8 @@
     cbuf,
     sxbuf,
     rxbuf,
-    szbuf,
-    rzbuf,
     zbuf,
     stat,
-    teach,
     load_sem,
     x_z,
     x_x,
@@ -53,8 +50,6 @@
     c_recv,
     rx_send,
     rx_recv,
-    rz_send,
-    rz_recv,
     z_z,
     z_x,
     z_c,
@@ -164,20 +159,19 @@
             for kx in range(1, n_col):
                 start(position, send_x.at[kz * n_col + kx], at(col_at(kx), core, ex))
 
-        to_columns(me, 0)
-        for kz in range(n_ex - 1, 0, -1):
-            start(me, send_z.at[kz], at(col, core, z_at(kz)))
+        def chips(order):
+            for kz in order:
+                for kx in range(n_col):
+                    if kz or kx:
+                        yield kz, kx
+
+        for kz, kx in chips(range(n_ex - 1, -1, -1)):
+            start(me, send_x.at[kz * n_col + kx], at(col_at(kx), core, z_at(kz)))
         start(me, send_c.at[0], sibling)
-        for kz in range(1, n_ex):
-            position = at(col, core, z_at(kz))
+        for kz, kx in chips(range(n_ex)):
+            position = at(col_at(n_col - kx), core, z_at(kz))
             arrive(position)
-            to_columns(position, kz)
-            start(position, send_c.at[kz * n_col], sibling)
-        for kz in range(n_ex):
-            for kx in range(1, n_col):
-                position = at(col_at(n_col - kx), core, z_at(kz))
-                arrive(position)
-                start(position, send_c.at[kz * n_col + kx], sibling)
+            start(position, send_c.at[kz * n_col + kx], sibling)
         for kz in range(n_ex):
             for kx in range(n_col):
                 arrive(at(col_at(n_col - kx), 1 - core, z_at(kz)))
@@ -239,40 +233,29 @@
     column_order = [*range(1, n_col), 0]
     for kx in column_order:
         half_sum(kx).start()
-    for kx in range(1, n_col):
+    for kx in column_order:
         half_sum(kx).wait_recv()
         sent.append(half_sum(kx))
-        for kz in range(n_ex - 1, -1, -1):
-            i = kx * n_ex + kz
-            sxbuf[i] = pair_sum(kx, kz).astype(BF16)
-            copy = remote(
-                sxbuf.at[i], rxbuf.at[i], rx_send.at[i], rx_recv.at[i], at(col_at(kx), core, ex)
-            )
-            copy.start()
-            sent.append(copy)
-    half_sum(0).wait_recv()
-    sent.append(half_sum(0))
-    mine = None
-    for kz in range(n_ex - 1, -1, -1):
-        mine = pair_sum(0, kz)
-        for kx in range(1, n_col):
-            i = kx * n_ex + kz
-            remote(
-                sxbuf.at[i], rxbuf.at[i], rx_send.at[i], rx_recv.at[i], at(col_at(kx), core, ex)
-            ).wait_recv()
-            mine += rxbuf[i].astype(F32)
-        if kz:
-            szbuf[kz] = mine.astype(BF16)
-            copy = remote(
-                szbuf.at[kz], rzbuf.at[kz], rz_send.at[kz], rz_recv.at[kz], at(col, core, z_at(kz))
-            )
-            copy.start()
-            sent.append(copy)
-    for kz in range(1, n_ex):
-        remote(
-            szbuf.at[kz], rzbuf.at[kz], rz_send.at[kz], rz_recv.at[kz], at(col, core, z_at(kz))
-        ).wait_recv()
-        mine += rzbuf[kz].astype(F32)
+
+    def scatter(kz, kx):
+        i = kx * n_ex + kz
+        return remote(
+            sxbuf.at[i],
+            rxbuf.at[i],
+            rx_send.at[i],
+            rx_recv.at[i],
+            at(col_at(kx), core, z_at(kz)),
+        )
+
+    order = [(kz, kx) for kz in range(n_ex - 1, -1, -1) for kx in column_order if kz or kx]
+    for kz, kx in order:
+        sxbuf[kx * n_ex + kz] = pair_sum(kx, kz).astype(BF16)
+        scatter(kz, kx).start()
+        sent.append(scatter(kz, kx))
+    mine = pair_sum(0, 0)
+    for kz, kx in reversed(order):
+        scatter(kz, kx).wait_recv()
+        mine += rxbuf[kx * n_ex + kz].astype(F32)
     mixed_low = x[:, :half] + mine[:per]
     mixed_top = x[:, half:] + mine[per:]
     square = jnp.sum(mixed_low * mixed_low + mixed_top * mixed_top, axis=-1, keepdims=True)
@@ -343,27 +326,40 @@
         log_s = s_top + jnp.log(s_total)
         divergence = cross / s_total - log_s + log_t
         valid = valid_ref[:, span].astype(F32)
-        kl_ref[:, span] = valid * divergence
+        for i, value in enumerate((log_s, divergence - log_t + log_s, valid, valid * divergence)):
+            facts[i : i + 1, span] = value
+        return carry
+
+    lax.fori_loop(0, total // rows, final, 0)
+
+    for copy in sent:
+        copy.wait_send()
+
+    def finish_tell(k, carry):
+        tell(k).wait_send()
+        return carry
+
+    lax.fori_loop(1, n_dev, finish_tell, 0)
+
+
+def finish(teach, st, facts, kl_ref, grad_ref):
+    total = teach.shape[0]
+    rows = min(total, 128)
+    kl_ref[...] = facts[3:4, :]
+
+    def part(r, carry):
+        span = pl.ds(pl.multiple_of(r * rows, rows), rows)
         where = lax.broadcasted_iota(jnp.int32, (LANES, rows), 0)
         table = jnp.zeros((LANES, rows), F32)
-        for i, value in enumerate((log_s, divergence - log_t + log_s, valid)):
-            table = jnp.where(where == i, value, table)
+        for i in range(3):
+            table = jnp.where(where == i, facts[i : i + 1, span], table)
         columns = table.T
         student = st[span, :].astype(F32)
         prob = columns[:, 2:3] * jnp.exp(student - columns[:, 0:1])
         grad_ref[span, :] = (prob * (student - teach[span, :] - columns[:, 1:2])).astype(BF16)
         return carry
 
-    lax.fori_loop(0, total // rows, final, 0)
-
-    for copy in sent:
-        copy.wait_send()
-
-    def finish_tell(k, carry):
-        tell(k).wait_send()
-        return carry
-
-    lax.fori_loop(1, n_dev, finish_tell, 0)
+    lax.fori_loop(0, total // rows, part, 0)
 
 
 def body(
@@ -392,11 +388,11 @@
     vmem = pl.BlockSpec(memory_space=pltpu.VMEM)
     hbm = pl.BlockSpec(memory_space=pl.ANY)
     dma = pltpu.SemaphoreType.DMA
-    kl, grad = pl.pallas_call(
+    teacher, facts = pl.pallas_call(
         functools.partial(kernel, n_dp, n_ex),
         out_shape=(
-            jax.ShapeDtypeStruct((1, total), F32),
-            jax.ShapeDtypeStruct((total, vocab), BF16),
+            jax.ShapeDtypeStruct((total, vocab), F32),
+            jax.ShapeDtypeStruct((4, total), F32),
         ),
         in_specs=[vmem] * 6 + [hbm] * 5,
         out_specs=(vmem, vmem),
@@ -412,11 +408,8 @@
             pltpu.VMEM((n_chip, 2 * per, half), BF16),
             pltpu.VMEM((n_chip, 2 * per, half), BF16),
             pltpu.VMEM((n_chip, 2 * per, half), BF16),
-            pltpu.VMEM((n_ex, 2 * per, half), BF16),
-            pltpu.VMEM((n_ex, 2 * per, half), BF16),
             pltpu.VMEM((n_dev, 2 * per, half), BF16),
             pltpu.VMEM((n_dev, 8, total), F32),
-            pltpu.VMEM((total, vocab), F32),
             dma((5,)),
             dma((n_ex,)),
             dma((n_chip,)),
@@ -426,8 +419,6 @@
             dma((n_col,)),
             dma((n_chip,)),
             dma((n_chip,)),
-            dma((n_ex,)),
-            dma((n_ex,)),
             dma((n_ex,)),
             dma((n_chip,)),
             dma((n_chip,)),
@@ -451,6 +442,16 @@
         head_weight,
         student_logits,
     )
+    kl, grad = pl.pallas_call(
+        finish,
+        out_shape=(
+            jax.ShapeDtypeStruct((1, total), F32),
+            jax.ShapeDtypeStruct((total, vocab), BF16),
+        ),
+        in_specs=[vmem] * 3,
+        out_specs=(vmem, vmem),
+        compiler_params=pltpu.CompilerParams(vmem_limit_bytes=24 * 2**20),
+    )(teacher, student_logits, facts)
     return kl.reshape(total), grad
 
 

time: 45 us -> 43.2 us (0.960)
  local copies, waits for them, and re-layouts: 2.73 us -> 1.62 us
  Pallas kernels: 41.4 us -> 40.7 us
    pallas_call x1, Pallas kernels: 41.4 us -> 39.8 us  [body(): pl.pallas_call(functools.partial(kernel, n_dp, n_ex), out_shape=(jax.Shap...]
    unnamed x2 -> x6, local copies, waits for them, and re-layouts: 2.73 us -> 1.62 us
    pallas_call x0 -> x1, Pallas kernels: none -> 0.91 us  [body(): pl.pallas_call(finish, out_shape=(jax.ShapeDtypeStruct((1, total), F32),...]
where the time goes in v3:
time: 43.2 us; the launch traced here: 43 us
  Pallas kernels  40.7 us (94%)
  local copies, waits for them, and re-layouts  1.62 us (4%)
  between operations  0.67 us (2%)
    pallas_call x1, Pallas kernels, body(): pl.pallas_call(functools.partial(kernel, n_dp, n_ex), out_shape=(jax.Shap...  39.8 us
    unnamed x6, local copies, waits for them, and re-layouts  1.62 us
    pallas_call x1, Pallas kernels, body(): pl.pallas_call(finish, out_shape=(jax.ShapeDtypeStruct((1, total), F32),...  0.91 us

profile of v3, /device:TPU:0, one launch (start us, length us, event | category | flops | bytes accessed | tf_op | source)
XLA Modules:
  0.0 43.0 jit_solution(9807856894017633984)
XLA Ops:
  0.6 0.0 copy-start
  0.6 39.8 %shard_map.122 = (f32[128,640]{1,0:T(8,128)}, f32[4,128]{1,0:T(4,128)}) custom-call(bf16[8,2048]{1,0:T(8,128)(2,1)} %tok_ref.1, s32[8,128]{1,0:T(8,128)} %bitcast.7, f32[8,8]{1,0:T(8,128)} %gates_ref.1, s32[1,128]{1,0:T(1,128)} %bitcast.8, f32[1,2048]{1,0:T(1,128)} %bitcast.5, f32[1,2048]{1,0:T(1,128)} %bitcast.6, bf16[4,2048,256]{2,1,0:T(8,128)(2,1)} %wg_hbm.1, ...), custom_call_target="tpu_custom_call" | custom-call | tf_op jit(solution)/shard_map/pallas_call | solution.py:391
  40.4 0.0 copy-done
  40.4 0.0 copy-start.1
  40.4 1.0 %copy-done.1 = f32[128,640]{1,0:T(8,128)S(1)} copy-done((f32[128,640]{1,0:T(8,128)S(1)}, f32[128,640]{1,0:T(8,128)}, u32[]{:S(2)}) %copy-start.1) | copy-done | bytes 327704
  41.4 0.0 copy-start.2
  41.4 0.7 %copy-done.2 = f32[4,128]{1,0:T(4,128)S(1)} copy-done((f32[4,128]{1,0:T(4,128)S(1)}, f32[4,128]{1,0:T(4,128)}, u32[]{:S(2)}) %copy-start.2) | copy-done | bytes 2072
  42.1 0.9 %shard_map.123 = (f32[1,128]{1,0:T(1,128)}, bf16[128,640]{1,0:T(8,128)(2,1)}) custom-call(f32[128,640]{1,0:T(8,128)S(1)} %copy-done.1, bf16[128,640]{1,0:T(8,128)(2,1)S(1)} %copy-done, f32[4,128]{1,0:T(4,128)S(1)} %copy-done.2), custom_call_target="tpu_custom_call" | custom-call | tf_op jit(solution)/shard_map/pallas_call | solution.py:445
Async XLA Ops:
  0.6 39.8 %copy-start = (bf16[128,640]{1,0:T(8,128)(2,1)S(1)}, bf16[128,640]{1,0:T(8,128)(2,1)}, u32[]{:S(2)}) copy-start(bf16[128,640]{1,0:T(8,128)(2,1)} %st.1) | copy-start | bytes 491524
  40.4 1.0 %copy-start.1 = (f32[128,640]{1,0:T(8,128)S(1)}, f32[128,640]{1,0:T(8,128)}, u32[]{:S(2)}) copy-start(f32[128,640]{1,0:T(8,128)} %get-tuple-element.6.teach) | copy-start | bytes 983044
  41.4 0.7 %copy-start.2 = (f32[4,128]{1,0:T(4,128)S(1)}, f32[4,128]{1,0:T(4,128)}, u32[]{:S(2)}) copy-start(f32[4,128]{1,0:T(4,128)} %get-tuple-element.7.facts) | copy-start | bytes 6148
